TPU v7x, 32 devices: a whole 2x2x4 slice. The times are simulated.
32 devices in a mesh: batch: 8 (over y, x, core), latent: 4 (over z).
Axes of the slice: x: 2, y: 2, z: 4, core: 2. Of those that a mesh axis runs over, the one named last changes fastest.
Arguments:
- rows: bfloat16 [4096, 2048], P('batch', 'latent'), may hold values from -8 to 8, as said below
- targets: bfloat16 [256, 2048], P('batch', 'latent'), may hold values from -16 to 16
- w_up: bfloat16 [2048, 1024], P('latent'), may hold values from -2.5 to 2.5
- bias: float32 [1024], replicated, may hold values from -3 to 3
- history: int32 [256, 512], P('batch'), may hold values from 0 to 511, as said below
- requests: int32 [64, 64], P('batch'), may hold values from -1 to 511, as said below
- upstream: bfloat16 [256, 1024], P('batch', 'latent'), may hold values from -6 to 6
Outputs:
- output: bfloat16 [256, 1024], P('batch', 'latent')
- row_grad: float32 [4096, 2048], P('batch', 'latent')
Inputs may be any that keep to these rules, and one draw needn't show every extreme that they name: `requests`: row d * 8 + o lists distinct owner-local row numbers in its first entries and -1 after them, with at least one live entry; for the last owner and for one owner drawn anew, every list is full. `history`: every entry names a live slot of its user's device. `rows`: values of order one.
All inputs are finite; a program needn't handle non-finite values.
Results may differ from a plain program's by a relative error of at most 0.012.
The roundings to bfloat16 on the way count: a program that leaves them out, or rounds other values in their place, can miss the bound.
Values may be sent and summed in bfloat16 or wider, within the bound.
No kernel may reach another device: no remote copies, remote signals or barrier semaphores. Data moves between devices by JAX's collectives and lax.ppermute only.
A program may use at most 64 MiB of HBM per device.

v0:
```python
import jax
import jax.numpy as jnp
from jax import lax
from jax.sharding import PartitionSpec as P

DL = 2048


def on_device(rows, targets, w_up, bias, history, requests, upstream):
    score_scale = DL ** (-0.5)
    owners = lax.axis_size("batch")
    capacity = requests.shape[1]
    slot_count = owners * capacity
    members = targets.shape[0]
    row_width = rows.shape[1]
    stored = rows.shape[0]
    hidden_share = upstream.shape[1]
    wanted = lax.all_to_all(requests, "batch", split_axis=0, concat_axis=0, tiled=True)
    usable = wanted >= 0
    chosen = jnp.take(rows, jnp.maximum(wanted, 0).reshape(-1), axis=0)
    chosen = jnp.where(usable.reshape(-1, 1), chosen, jnp.zeros_like(chosen))
    arrived = lax.all_to_all(
        chosen.reshape(owners, capacity, row_width),
        "batch",
        split_axis=0,
        concat_axis=0,
        tiled=True,
    )
    fetched = arrived.reshape(slot_count, row_width)
    offsets = (jnp.arange(members, dtype=jnp.int32) * slot_count)[:, None]
    segment_ids = (history + offsets).reshape(-1)

    def slot_sums(values):
        return jax.ops.segment_sum(values.reshape(-1), segment_ids, members * slot_count).reshape(
            members, slot_count
        )

    slot_scores = jnp.einsum("ud,sd->us", targets, fetched, preferred_element_type=jnp.float32)
    whole_scores = lax.psum(slot_scores, "latent")
    scores = jnp.take_along_axis(whole_scores, history, axis=1) * score_scale
    probability = jax.nn.softmax(scores, axis=1)
    weight = slot_sums(probability)
    pooled = jnp.dot(
        weight.astype(jnp.bfloat16), fetched, preferred_element_type=jnp.float32
    ).astype(jnp.bfloat16)
    partial_hidden = jnp.dot(pooled, w_up, preferred_element_type=jnp.float32)
    column = lax.axis_index("latent") * hidden_share
    hidden = lax.psum_scatter(partial_hidden, "latent", scatter_dimension=1, tiled=True)
    hidden = hidden + lax.dynamic_slice_in_dim(bias, column, hidden_share)
    activated, backward = jax.vjp(jax.nn.gelu, hidden)
    output = activated.astype(jnp.bfloat16)
    slopes = backward(upstream.astype(jnp.float32))[0].astype(jnp.bfloat16)
    slopes_full = lax.all_gather(slopes, "latent", axis=1, tiled=True)
    pooled_grad = jnp.einsum("uh,dh->ud", slopes_full, w_up, preferred_element_type=jnp.float32)
    slot_slopes = jnp.einsum(
        "ud,sd->us", pooled_grad.astype(jnp.bfloat16), fetched, preferred_element_type=jnp.float32
    )
    whole_slopes = lax.psum(slot_slopes, "latent")
    probability_grad = jnp.take_along_axis(whole_slopes, history, axis=1)
    score_grad = probability * (
        probability_grad - jnp.sum(probability * probability_grad, axis=1, keepdims=True)
    )
    weight_grad = slot_sums(score_grad)
    destination = jnp.where(usable, wanted, stored)
    slot_grad = jnp.einsum("us,ud->sd", weight, pooled_grad, precision=lax.Precision.HIGHEST)
    slot_grad = slot_grad + score_scale * jnp.einsum(
        "us,ud->sd", weight_grad, targets.astype(jnp.float32), precision=lax.Precision.HIGHEST
    )
    returned = lax.all_to_all(
        slot_grad.reshape(owners, capacity, row_width),
        "batch",
        split_axis=0,
        concat_axis=0,
        tiled=True,
    )
    summed = jax.ops.segment_sum(
        returned.reshape(-1, row_width), destination.reshape(-1), stored + 1
    )
    return (output, summed[:stored])


def solution(mesh):
    return jax.shard_map(
        on_device,
        mesh=mesh,
        in_specs=(
            P("batch", "latent"),
            P("batch", "latent"),
            P("latent", None),
            P(),
            P("batch", None),
            P("batch", None),
            P("batch", "latent"),
        ),
        out_specs=(P("batch", "latent"), P("batch", "latent")),
        check_vma=False,
    )
```

profile of v0, /device:TPU:0, one launch (start us, length us, event | category | flops | bytes accessed | tf_op | source)
XLA Modules:
  0.0 615.2 jit_solution(12138111015020188799)
XLA Ops:
  7.2 0.0 copy-start
  7.2 9.9 %all_to_all.22 = s32[8,1,64]{2,1,0:T(1,128)S(1)} all-to-all(s32[8,1,64]{2,1,0:T(1,128)} %bitcast.59), channel_id=1, replica_groups=mesh['batch'=8,'latent'=4] {'batch'}, dimensions={0} | all-to-all | bytes 4096 | tf_op jit(solution)/shard_map/all_to_all | solution.py:18
  17.1 0.5 broadcast.171
  17.6 0.7 reduce.3
  18.3 0.1 all_to_all.16
  18.4 3.1 gather_fusion
  21.5 0.0 copy-start.1
  21.5 0.0 copy-start.2
  21.5 1.0 select_select_fusion
  22.5 3.5 all-to-all-start.1
  26.0 0.0 all-reduce.3.cloned.1.call-start
  26.0 0.0 copy-done.1
  26.1 0.1 add_bitcast_fusion
  26.1 9.5 %all-to-all-done.1 = bf16[8,64,512]{2,1,0:T(8,128)(2,1)S(1)} async-done(((bf16[8,64,512]{2,1,0:T(8,128)(2,1)}), bf16[8,64,512]{2,1,0:T(8,128)(2,1)S(1)}, u32[]{:S(2)}, u32[]{:S(2)}) %all-to-all-start.1) | async-done | bytes 524320 | tf_op jit(solution)/shard_map/all_to_all | solution.py:22
  35.7 0.0 copy-done.2
  35.7 0.9 convolution_bitcast_fusion
  36.6 0.0 all-reduce.3.cloned.1.call-update
  36.6 0.0 reduce-scatter.2.cloned.1.call-start
  36.7 33.4 %all-reduce.3.cloned.1.call-done = f32[32,512]{1,0:T(8,128)} async-done(((f32[32,512]{1,0:T(8,128)}), f32[32,512]{1,0:T(8,128)}) %all-reduce.3.cloned.1.call-update) | async-done | bytes 65552 | tf_op jit(solution)/shard_map/psum | solution.py:39
  70.1 108.9 %gather_fusion.1 = f32[16384]{0:T(1024)S(1)} fusion(f32[32,512]{1,0:T(8,128)} %all-reduce.3.cloned.1.call-done, s32[16384]{0:T(1024)S(1)} %bitcast.45), kind=kCustom, calls=%fused_computation.clone | custom fusion | bytes 262144 | tf_op jit(solution)/shard_map/jit(take_along_axis)/gather | solution.py:40
  179.0 0.1 fusion.7
  179.1 0.2 fusion.6
  179.3 0.1 fusion.25
  179.5 113.5 %scatter_custom_fusion = f32[16384]{0:T(1024)S(1)} fusion(s32[16384]{0:T(1024)S(1)} %bitcast.53, f32[16384]{0:T(1024)S(1)} %bitcast.56, f32[]{:T(128)} %constant.25.clone.1), kind=kCustom, calls=%fused_computation.46 | custom fusion | flops 16384 | bytes 65540 | tf_op jit(solution)/shard_map/scatter-add | solution.py:34
  293.0 0.0 copy-start.3
  293.0 0.0 copy-done
  293.0 1.1 fusion.1
  294.1 0.0 reduce-scatter.2.cloned.1.call-update
  294.2 0.0 all-reduce.5.cloned.1.call-start
  294.2 0.8 dynamic_slice.3
  295.0 18.2 %reduce-scatter.2.cloned.1.call-done = f32[32,256]{1,0:T(8,128)} async-done(((f32[32,1024]{1,0:T(8,128)}), f32[32,256]{1,0:T(8,128)}) %reduce-scatter.2.cloned.1.call-update) | async-done | bytes 32784 | tf_op jit(solution)/shard_map/reduce_scatter | solution.py:48
  313.2 0.0 copy-done.3
  313.2 1.4 fusion.10
  314.6 13.1 %all_gather.3 = bf16[32,1024]{1,0:T(8,128)(2,1)S(1)} all-gather(bf16[32,256]{1,0:T(8,128)(2,1)S(1)} %get-tuple-element.5), channel_id=1, replica_groups=mesh['batch'=8,'latent'=4] {'latent'}, dimensions={1}, use_global_device_ids=true | all-gather | bytes 81920 | tf_op jit(solution)/shard_map/all_gather | solution.py:53
  327.7 0.4 fusion.26
  328.1 0.9 fusion.18
  329.1 0.0 all-reduce.5.cloned.1.call-update
  329.1 1.0 fusion.27
  330.1 31.3 %all-reduce.5.cloned.1.call-done = f32[32,512]{1,0:T(8,128)} async-done(((f32[32,512]{1,0:T(8,128)}), f32[32,512]{1,0:T(8,128)}) %all-reduce.5.cloned.1.call-update) | async-done | bytes 65552 | tf_op jit(solution)/shard_map/psum | solution.py:58
  361.4 108.9 %gather_fusion.2 = f32[16384]{0:T(1024)S(1)} fusion(f32[32,512]{1,0:T(8,128)} %all-reduce.5.cloned.1.call-done, s32[16384]{0:T(1024)S(1)} %bitcast.46), kind=kCustom, calls=%fused_computation.1.clone | custom fusion | bytes 262144 | tf_op jit(solution)/shard_map/jit(take_along_axis)/gather | solution.py:59
  470.3 0.2 multiply_reduce_fusion
  470.5 0.1 multiply_bitcast_fusion
  470.6 113.5 %scatter_custom_fusion.1 = f32[16384]{0:T(1024)S(1)} fusion(s32[16384]{0:T(1024)S(1)} %bitcast.54, f32[16384]{0:T(1024)S(1)} %bitcast.55, f32[]{:T(128)} %constant.25.clone.1), kind=kCustom, calls=%fused_computation.44 | custom fusion | flops 16384 | bytes 65540 | tf_op jit(solution)/shard_map/scatter-add | solution.py:34
  584.2 0.7 fusion
  584.8 18.8 %all_to_all.23 = f32[8,64,512]{2,1,0:T(8,128)S(1)} all-to-all(f32[8,64,512]{2,1,0:T(8,128)S(1)} %bitcast.50), channel_id=1, replica_groups=mesh['batch'=8,'latent'=4] {'batch'}, dimensions={0} | all-to-all | bytes 2097152 | tf_op jit(solution)/shard_map/all_to_all | solution.py:69
  603.6 4.0 scatter_custom_fusion.2
  607.6 1.0 slice.10
  (15 shorter events, 0.2 us)
Async XLA Ops:
  7.2 285.9 %copy-start = (bf16[512,1024]{1,0:T(8,128)(2,1)S(1)}, bf16[512,1024]{1,0:T(8,128)(2,1)}, u32[]{:S(2)}) copy-start(bf16[512,1024]{1,0:T(8,128)(2,1)} %param.11) | copy-start | bytes 3145732
  21.5 4.6 copy-start.1
  21.5 14.2 %copy-start.2 = (bf16[32,512]{1,0:T(8,128)(2,1)S(1)}, bf16[32,512]{1,0:T(8,128)(2,1)}, u32[]{:S(2)}) copy-start(bf16[32,512]{1,0:T(8,128)(2,1)} %param.10) | copy-start | bytes 98308
  22.5 13.2 %all-to-all-start.1 = ((bf16[8,64,512]{2,1,0:T(8,128)(2,1)}), bf16[8,64,512]{2,1,0:T(8,128)(2,1)S(1)}, u32[]{:S(2)}, u32[]{:S(2)}) async-start(bf16[8,64,512]{2,1,0:T(8,128)(2,1)} %select_select_fusion), calls=%async_computation.1 | async-start | bytes 1048576 | tf_op jit(solution)/shard_map/all_to_all | solution.py:22
  26.0 44.1 %all-reduce.3.cloned.1.call-start = ((), (), s32[]{:S(2)}) async-start(), calls=%async_computation.4 | async-start | bytes 131072 | tf_op jit(solution)/shard_map/psum | solution.py:39
  36.6 276.6 %reduce-scatter.2.cloned.1.call-start = ((), (), s32[]{:S(2)}) async-start(), calls=%async_computation.5 | async-start | bytes 163840 | tf_op jit(solution)/shard_map/reduce_scatter | solution.py:48
  293.0 20.2 %copy-start.3 = (bf16[32,256]{1,0:T(8,128)(2,1)S(1)}, bf16[32,256]{1,0:T(8,128)(2,1)}, u32[]{:S(2)}) copy-start(bf16[32,256]{1,0:T(8,128)(2,1)} %param.15) | copy-start | bytes 49156
  294.2 67.2 %all-reduce.5.cloned.1.call-start = ((), (), s32[]{:S(2)}) async-start(), calls=%async_computation.6 | async-start | bytes 131072 | tf_op jit(solution)/shard_map/psum | solution.py:58
Sparse Core Ops, SparseCore 0:
  36.7 33.3 all-reduce.2
  294.3 18.8 reduce-scatter.1
  329.2 32.1 all-reduce.4
where the time goes:
time: 616 us; the launch traced here: 615 us
  other arithmetic  235 us (38%)
  local copies, waits for them, and re-layouts  223 us (36%)
  waiting for transfers between devices  92.5 us (15%)
  blocking collectives  41.8 us (7%)
  between operations  14 us (2%)
    scatter-add x2, other arithmetic, slot_sums(): jax.ops.segment_sum(values.reshape(-1), segment_ids, members * slot_count)  227 us
    gather x2, local copies, waits for them, and re-layouts, on_device(): scores = jnp.take_along_axis(whole_scores, history, axis=1) * score_scale  109 us
    gather x2, local copies, waits for them, and re-layouts, on_device(): probability_grad = jnp.take_along_axis(whole_slopes, history, axis=1)  109 us
    psum x1, waiting for transfers between devices, on_device(): whole_scores = lax.psum(slot_scores, 'latent')  33.4 us
    psum x1, waiting for transfers between devices, on_device(): whole_slopes = lax.psum(slot_slopes, 'latent')  31.3 us
    all_to_all x1, blocking collectives, on_device(): lax.all_to_all(slot_grad.reshape(owners, capacity, row_width), 'batch', s...  18.8 us
    reduce_scatter x1, waiting for transfers between devices, on_device(): lax.psum_scatter(partial_hidden, 'latent', scatter_dimension=1, tiled=True)  18.2 us
    all_gather x1, blocking collectives, on_device(): slopes_full = lax.all_gather(slopes, 'latent', axis=1, tiled=True)  13.1 us
  transfers between devices with their start and end apart: 4, of which 4 were waited for; matrix products, arithmetic and copies ran while one was open for 0% of the time, Pallas kernels for 0%

commit v1 on v0

--- a/solution.py
+++ b/solution.py
@@ -55,7 +55,11 @@
     slot_slopes = jnp.einsum(
         "ud,sd->us", pooled_grad.astype(jnp.bfloat16), fetched, preferred_element_type=jnp.float32
     )
-    whole_slopes = lax.psum(slot_slopes, "latent")
+    whole_slopes = slot_slopes
+    for hop in (1, 2):
+        whole_slopes = whole_slopes + lax.ppermute(
+            whole_slopes, "latent", [(dev, dev ^ hop) for dev in range(4)]
+        )
     probability_grad = jnp.take_along_axis(whole_slopes, history, axis=1)
     score_grad = probability * (
         probability_grad - jnp.sum(probability * probability_grad, axis=1, keepdims=True)

time: 616 us -> 613 us (level)
  waiting for transfers between devices: 92.5 us -> 69.2 us
  local copies, waits for them, and re-layouts: 223 us -> 244 us
    psum x1 -> x0, waiting for transfers between devices: 31.3 us -> none  [on_device(): whole_slopes = lax.psum(slot_slopes, 'latent')]
    gather x2, local copies, waits for them, and re-layouts: 109 us -> 129 us  [on_device(): probability_grad = jnp.take_along_axis(whole_slopes, history, axis=1)]
    ppermute x0 -> x2, waiting for transfers between devices: none -> 7.94 us  [on_device(): lax.ppermute(whole_slopes, 'latent', [(dev, dev ^ hop) for dev in range(4)])]
  transfers between devices with their start and end apart: 4 -> 5, of which waited for: 4 -> 5; matrix products, arithmetic and copies ran while one was open for 0% -> 0% of each run, Pallas kernels for 0% -> 0%
where the time goes in v1:
time: 613 us
  local copies, waits for them, and re-layouts  244 us (40%)
  other arithmetic  235 us (38%)
  waiting for transfers between devices  69.2 us (11%)
  blocking collectives  41.8 us (7%)
  between operations  14.3 us (2%)
    scatter-add x2, other arithmetic, slot_sums(): jax.ops.segment_sum(values.reshape(-1), segment_ids, members * slot_count)  227 us
    gather x2, local copies, waits for them, and re-layouts, on_device(): probability_grad = jnp.take_along_axis(whole_slopes, history, axis=1)  129 us
    gather x2, local copies, waits for them, and re-layouts, on_device(): scores = jnp.take_along_axis(whole_scores, history, axis=1) * score_scale  109 us
    psum x1, waiting for transfers between devices, on_device(): whole_scores = lax.psum(slot_scores, 'latent')  33.4 us
    all_to_all x1, blocking collectives, on_device(): lax.all_to_all(slot_grad.reshape(owners, capacity, row_width), 'batch', s...  18.8 us
    reduce_scatter x1, waiting for transfers between devices, on_device(): lax.psum_scatter(partial_hidden, 'latent', scatter_dimension=1, tiled=True)  18.3 us
    all_gather x1, blocking collectives, on_device(): slopes_full = lax.all_gather(slopes, 'latent', axis=1, tiled=True)  13.1 us
  transfers between devices with their start and end apart: 5, of which 5 were waited for; matrix products, arithmetic and copies ran while one was open for 0% of the time, Pallas kernels for 0%

profile of v1, /device:TPU:0, one launch (start us, length us, event | category | flops | bytes accessed | tf_op | source)
XLA Modules:
  0.0 612.8 jit_solution(4246375329917608825)
XLA Ops:
  7.2 0.0 copy-start
  7.2 9.9 %all_to_all.22 = s32[8,1,64]{2,1,0:T(1,128)S(1)} all-to-all(s32[8,1,64]{2,1,0:T(1,128)} %bitcast.59), channel_id=1, replica_groups=mesh['batch'=8,'latent'=4] {'batch'}, dimensions={0} | all-to-all | bytes 4096 | tf_op jit(solution)/shard_map/all_to_all | solution.py:18
  17.1 0.5 broadcast.171
  17.6 0.7 reduce.3
  18.3 0.1 all_to_all.16
  18.4 3.1 gather_fusion
  21.5 0.0 copy-start.1
  21.5 0.0 copy-start.2
  21.5 1.0 select_select_fusion
  22.5 3.5 all-to-all-start.1
  26.0 0.0 all-reduce.2.cloned.1.call-start
  26.0 0.0 copy-done.1
  26.1 0.1 add_bitcast_fusion
  26.1 9.5 %all-to-all-done.1 = bf16[8,64,512]{2,1,0:T(8,128)(2,1)S(1)} async-done(((bf16[8,64,512]{2,1,0:T(8,128)(2,1)}), bf16[8,64,512]{2,1,0:T(8,128)(2,1)S(1)}, u32[]{:S(2)}, u32[]{:S(2)}) %all-to-all-start.1) | async-done | bytes 524320 | tf_op jit(solution)/shard_map/all_to_all | solution.py:22
  35.7 0.0 copy-done.2
  35.7 0.9 convolution_bitcast_fusion
  36.6 0.0 all-reduce.2.cloned.1.call-update
  36.6 0.0 reduce-scatter.2.cloned.1.call-start
  36.7 33.4 %all-reduce.2.cloned.1.call-done = f32[32,512]{1,0:T(8,128)} async-done(((f32[32,512]{1,0:T(8,128)}), f32[32,512]{1,0:T(8,128)}) %all-reduce.2.cloned.1.call-update) | async-done | bytes 65552 | tf_op jit(solution)/shard_map/psum | solution.py:39
  70.1 108.9 %gather_fusion.1 = f32[16384]{0:T(1024)S(1)} fusion(f32[32,512]{1,0:T(8,128)} %all-reduce.2.cloned.1.call-done, s32[16384]{0:T(1024)S(1)} %bitcast.45), kind=kCustom, calls=%fused_computation.clone | custom fusion | bytes 262144 | tf_op jit(solution)/shard_map/jit(take_along_axis)/gather | solution.py:40
  179.0 0.1 fusion.7
  179.1 0.2 fusion.6
  179.3 0.1 fusion.25
  179.5 0.0 copy-start.3
  179.5 113.5 %scatter_custom_fusion = f32[16384]{0:T(1024)S(1)} fusion(s32[16384]{0:T(1024)S(1)} %bitcast.53, f32[16384]{0:T(1024)S(1)} %bitcast.56, f32[]{:T(128)} %constant.25.clone.1), kind=kCustom, calls=%fused_computation.46 | custom fusion | flops 16384 | bytes 65540 | tf_op jit(solution)/shard_map/scatter-add | solution.py:34
  293.0 0.0 copy-done
  293.0 1.1 fusion.1
  294.1 0.0 reduce-scatter.2.cloned.1.call-update
  294.2 0.8 dynamic_slice.3
  294.9 18.3 %reduce-scatter.2.cloned.1.call-done = f32[32,256]{1,0:T(8,128)} async-done(((f32[32,1024]{1,0:T(8,128)}), f32[32,256]{1,0:T(8,128)}) %reduce-scatter.2.cloned.1.call-update) | async-done | bytes 32784 | tf_op jit(solution)/shard_map/reduce_scatter | solution.py:48
  313.2 0.0 copy-done.3
  313.2 1.4 fusion.10
  314.6 13.1 %all_gather.3 = bf16[32,1024]{1,0:T(8,128)(2,1)S(1)} all-gather(bf16[32,256]{1,0:T(8,128)(2,1)S(1)} %get-tuple-element.5), channel_id=1, replica_groups=mesh['batch'=8,'latent'=4] {'latent'}, dimensions={1}, use_global_device_ids=true | all-gather | bytes 81920 | tf_op jit(solution)/shard_map/all_gather | solution.py:53
  327.7 0.4 fusion.26
  328.1 0.3 fusion.18
  328.4 0.0 collective-permute-start
  328.4 4.2 collective-permute-done
  332.7 0.7 collective-permute-start.1
  333.4 1.0 fusion.27
  334.4 3.7 collective-permute-done.1
  338.1 129.5 %gather_fusion.2 = f32[16384]{0:T(1024)S(1)} fusion(f32[32,512]{1,0:T(8,128)S(1)} %add.66, s32[16384]{0:T(1024)S(1)} %bitcast.46), kind=kCustom, calls=%fused_computation.1.clone | custom fusion | bytes 262144 | tf_op jit(solution)/shard_map/jit(take_along_axis)/gather | solution.py:63
  467.6 0.2 multiply_reduce_fusion
  467.8 0.1 multiply_bitcast_fusion
  467.9 113.5 %scatter_custom_fusion.1 = f32[16384]{0:T(1024)S(1)} fusion(s32[16384]{0:T(1024)S(1)} %bitcast.54, f32[16384]{0:T(1024)S(1)} %bitcast.55, f32[]{:T(128)} %constant.25.clone.1), kind=kCustom, calls=%fused_computation.44 | custom fusion | flops 16384 | bytes 65540 | tf_op jit(solution)/shard_map/scatter-add | solution.py:34
  581.4 0.7 fusion
  582.1 18.8 %all_to_all.23 = f32[8,64,512]{2,1,0:T(8,128)S(1)} all-to-all(f32[8,64,512]{2,1,0:T(8,128)S(1)} %bitcast.50), channel_id=1, replica_groups=mesh['batch'=8,'latent'=4] {'batch'}, dimensions={0} | all-to-all | bytes 2097152 | tf_op jit(solution)/shard_map/all_to_all | solution.py:73
  600.9 4.0 scatter_custom_fusion.2
  604.9 1.0 slice.10
  (17 shorter events, 0.2 us)
Async XLA Ops:
  7.2 285.9 %copy-start = (bf16[512,1024]{1,0:T(8,128)(2,1)S(1)}, bf16[512,1024]{1,0:T(8,128)(2,1)}, u32[]{:S(2)}) copy-start(bf16[512,1024]{1,0:T(8,128)(2,1)} %param.11) | copy-start | bytes 3145732
  21.5 4.6 copy-start.1
  21.5 14.2 %copy-start.2 = (bf16[32,512]{1,0:T(8,128)(2,1)S(1)}, bf16[32,512]{1,0:T(8,128)(2,1)}, u32[]{:S(2)}) copy-start(bf16[32,512]{1,0:T(8,128)(2,1)} %param.10) | copy-start | bytes 98308
  22.5 13.2 %all-to-all-start.1 = ((bf16[8,64,512]{2,1,0:T(8,128)(2,1)}), bf16[8,64,512]{2,1,0:T(8,128)(2,1)S(1)}, u32[]{:S(2)}, u32[]{:S(2)}) async-start(bf16[8,64,512]{2,1,0:T(8,128)(2,1)} %select_select_fusion), calls=%async_computation.1 | async-start | bytes 1048576 | tf_op jit(solution)/shard_map/all_to_all | solution.py:22
  26.0 44.1 %all-reduce.2.cloned.1.call-start = ((), (), s32[]{:S(2)}) async-start(), calls=%async_computation.4 | async-start | bytes 131072 | tf_op jit(solution)/shard_map/psum | solution.py:39
  36.6 276.6 %reduce-scatter.2.cloned.1.call-start = ((), (), s32[]{:S(2)}) async-start(), calls=%async_computation.5 | async-start | bytes 163840 | tf_op jit(solution)/shard_map/reduce_scatter | solution.py:48
  179.5 133.8 %copy-start.3 = (bf16[32,256]{1,0:T(8,128)(2,1)S(1)}, bf16[32,256]{1,0:T(8,128)(2,1)}, u32[]{:S(2)}) copy-start(bf16[32,256]{1,0:T(8,128)(2,1)} %param.15) | copy-start | bytes 49156
  328.4 4.3 collective-permute-start
  332.7 5.4 collective-permute-start.1
Sparse Core Ops, SparseCore 0:
  36.7 33.3 all-reduce.1
  294.3 18.8 reduce-scatter.1
